TPU v7x, 32 devices: a whole 2x2x4 slice. The times are simulated.
32 devices in a mesh: dom: 8 (over z, y), tile: 4 (over x, core).
Axes of the slice: x: 2, y: 2, z: 4, core: 2. Of those that a mesh axis runs over, the one named last changes fastest.
Arguments:
- features: bfloat16 [16384, 256], P(('dom', 'tile')), may hold values from -6 to 6
- grad_out: bfloat16 [16384, 256], P(('dom', 'tile')), may hold values from -6 to 6
- self_weight: bfloat16 [256, 256], replicated, may hold values from -0.375 to 0.375
- neigh_weight: bfloat16 [256, 256], replicated, may hold values from -0.375 to 0.375
- edge_tiles: bfloat16 [2304, 128, 128], P(('dom', 'tile')), may hold values from 0 to 1.5, as said below
- tile_dst: int32 [2304], P(('dom', 'tile')), may hold values from 0 to 15
- tile_src: int32 [2304], P(('dom', 'tile')), may hold values from 0 to 25
- halo_send: int32 [8, 1024], P('dom'), may hold values from 0 to 2047
- hub_ids: int32 [256], P('dom'), may hold values from 0 to 2047
Outputs:
- activated: bfloat16 [16384, 256], P(('dom', 'tile'))
- grad_features: bfloat16 [16384, 256], P(('dom', 'tile'))
- grad_self_weight: float32 [256, 256], replicated
- grad_neigh_weight: float32 [256, 256], replicated
Inputs may be any that keep to these rules, and one draw needn't show every extreme that they name: `edge_tiles`: each entry is zero or an edge weight of 0.3 or more.
All inputs are finite; a program needn't handle non-finite values.
Results may differ from a plain program's by a relative error of at most 0.014.
Values may be sent and summed in bfloat16 or wider, within the bound.
A program may use at most 64 MiB of HBM per device.

v0:
```python
import jax
import jax.numpy as jnp
from jax import lax
from jax.sharding import PartitionSpec as P


def block_onehot(indices, number):
    return (indices[None, :] == jnp.arange(number, dtype=jnp.int32)[:, None]).astype(jnp.float32)


def on_device(
    features,
    grad_out,
    self_weight,
    neigh_weight,
    edge_tiles,
    tile_dst,
    tile_src,
    halo_send,
    hub_ids,
):
    domains = lax.axis_size("dom")
    groups = lax.axis_size("tile")
    quarter = features.shape[0]
    columns = features.shape[1]
    tile_size = edge_tiles.shape[1]
    halo_total = halo_send.shape[1]
    per_peer = halo_total // domains
    whole_rows = lax.all_gather(features, "tile", axis=0, tiled=True)
    vertices = whole_rows.shape[0]
    outgoing = whole_rows[halo_send[0]].reshape(domains, per_peer, columns)
    own_hubs = whole_rows[hub_ids]
    width = outgoing.shape[2]
    halo_rows = lax.all_to_all(outgoing, "dom", split_axis=0, concat_axis=0, tiled=True).reshape(
        halo_total, width
    )
    hub_rows = lax.all_gather(own_hubs, "dom", axis=0, tiled=True)
    boundary = jnp.concatenate([halo_rows, hub_rows], axis=0)
    source = jnp.concatenate([whole_rows, boundary], axis=0)
    src_rows = source.shape[0]
    src_blocks = src_rows // tile_size
    dst_blocks = vertices // tile_size
    picked = source.reshape(src_blocks, tile_size, columns)[tile_src]
    products = jnp.einsum("tij,tjf->tif", edge_tiles, picked, preferred_element_type=jnp.float32)
    into_dest = block_onehot(tile_dst, dst_blocks)
    partial_sum = jnp.einsum(
        "dt,tif->dif", into_dest, products, precision=lax.Precision.HIGHEST
    ).reshape(vertices, columns)
    row_weight = jnp.sum(edge_tiles, axis=2, dtype=jnp.float32)
    partial_degree = jnp.dot(into_dest, row_weight, precision=lax.Precision.HIGHEST).reshape(
        vertices
    )
    summed, degree = (
        lax.psum_scatter(
            partial_sum.astype(jnp.bfloat16), "tile", scatter_dimension=0, tiled=True
        ).astype(jnp.float32),
        lax.psum_scatter(
            partial_degree.astype(jnp.bfloat16), "tile", scatter_dimension=0, tiled=True
        ).astype(jnp.float32),
    )
    divisor = jnp.maximum(degree, 1.0)
    mean_rows = (summed / divisor[:, None]).astype(jnp.bfloat16)
    hidden = jnp.dot(features, self_weight, preferred_element_type=jnp.float32) + jnp.dot(
        mean_rows, neigh_weight, preferred_element_type=jnp.float32
    )
    activated = jax.nn.silu(hidden).astype(jnp.bfloat16)
    sigmoid_h = jax.nn.sigmoid(hidden)
    grad_hidden = (
        grad_out.astype(jnp.float32) * sigmoid_h * (1.0 + hidden * (1.0 - sigmoid_h))
    ).astype(jnp.bfloat16)
    self_term = jnp.einsum("nf,nh->fh", features, grad_hidden, preferred_element_type=jnp.float32)
    neigh_term = jnp.einsum("nf,nh->fh", mean_rows, grad_hidden, preferred_element_type=jnp.float32)
    grad_self_sum, grad_neigh_sum = lax.psum((self_term, neigh_term), ("dom", "tile"))
    inv_root = 1.0 / (quarter * groups * domains) ** 0.5
    grad_mean = lax.dot_general(
        grad_hidden, neigh_weight, (((1,), (1,)), ((), ())), preferred_element_type=jnp.float32
    )
    grad_mean_b = (grad_mean / divisor[:, None]).astype(jnp.bfloat16)
    grad_whole = lax.all_gather(grad_mean_b, "tile", axis=0, tiled=True)
    dst_pick = grad_whole.reshape(dst_blocks, tile_size, columns)[tile_dst]
    back_prod = jnp.einsum("tij,tif->tjf", edge_tiles, dst_pick, preferred_element_type=jnp.float32)
    into_source = block_onehot(tile_src, src_blocks)
    partial_src = jnp.einsum(
        "st,tjf->sjf", into_source, back_prod, precision=lax.Precision.HIGHEST
    ).reshape(src_rows, columns)
    grad_local = lax.psum_scatter(
        partial_src[:vertices].astype(jnp.bfloat16), "tile", scatter_dimension=0, tiled=True
    ).astype(jnp.float32)
    remote = lax.psum(partial_src[vertices:].astype(jnp.bfloat16), "tile").astype(jnp.float32)
    halo_grad = remote[:halo_total].reshape(domains, per_peer, width)
    hub_grad = remote[halo_total:]
    halo_back = (
        lax.all_to_all(
            halo_grad.astype(jnp.bfloat16), "dom", split_axis=0, concat_axis=0, tiled=True
        )
        .astype(halo_grad.dtype)
        .reshape(halo_total, width)
    )
    hub_back = lax.psum_scatter(hub_grad, "dom", scatter_dimension=0, tiled=True)
    spread = jnp.zeros((vertices, width), jnp.float32).at[halo_send[0]].add(halo_back)
    spread = spread.at[hub_ids].add(hub_back)
    own_spread = lax.dynamic_slice_in_dim(spread, lax.axis_index("tile") * quarter, quarter, 0)
    grad_features = (
        lax.dot_general(
            grad_hidden, self_weight, (((1,), (1,)), ((), ())), preferred_element_type=jnp.float32
        )
        + grad_local
        + own_spread
    )
    return (
        activated,
        grad_features.astype(jnp.bfloat16),
        grad_self_sum * inv_root,
        grad_neigh_sum * inv_root,
    )


def solution(mesh):
    return jax.shard_map(
        on_device,
        mesh=mesh,
        in_specs=(
            P(("dom", "tile"), None),
            P(("dom", "tile"), None),
            P(),
            P(),
            P(("dom", "tile"), None, None),
            P(("dom", "tile")),
            P(("dom", "tile")),
            P("dom", None),
            P("dom"),
        ),
        out_specs=(P(("dom", "tile"), None), P(("dom", "tile"), None), P(), P()),
        check_vma=False,
    )
```

profile of v0, /device:TPU:0, one launch (start us, length us, event | category | flops | bytes accessed | tf_op | source)
XLA Modules:
  0.0 453.9 jit_solution(10285785023682862956)
XLA Ops:
  7.2 0.0 copy-start
  7.2 0.0 copy-start.9
  7.2 0.0 all-gather.4.cloned.1.call-start
  7.3 0.7 all-gather.4.cloned.1.call-update
  7.9 0.7 compare_select_fusion
  8.6 20.4 %all-gather.4.cloned.1.call-done = bf16[2048,256]{1,0:T(8,128)(2,1)} async-done(((bf16[512,256]{1,0:T(8,128)(2,1)}), bf16[2048,256]{1,0:T(8,128)(2,1)}) %all-gather.4.cloned.1.call-update) | async-done | bytes 1048592 | tf_op jit(solution)/shard_map/all_gather | solution.py:29
  29.1 6.0 %gather_fusion = bf16[1024,256]{1,0:T(8,128)(2,1)} fusion(bf16[2048,256]{1,0:T(8,128)(2,1)} %all-gather.4.cloned.1.call-done, s32[1024]{0:T(1024)S(1)} %broadcast_clamp_fusion), kind=kCustom, calls=%fused_computation | custom fusion | bytes 1052672 | tf_op jit(solution)/shard_map/gather | solution.py:31
  35.1 5.5 %all-to-all-start = ((bf16[8,128,256]{2,1,0:T(8,128)(2,1)}), bf16[8,128,256]{2,1,0:T(8,128)(2,1)S(1)}, u32[]{:S(2)}, u32[]{:S(2)}) async-start(bf16[8,128,256]{2,1,0:T(8,128)(2,1)} %bitcast.3), calls=%async_computation | async-start | bytes 1048576 | tf_op jit(solution)/shard_map/all_to_all | solution.py:34
  40.6 0.0 reduce-scatter.4.cloned.1.call-start
  40.7 0.6 gather_fusion.1
  41.4 36.8 %all-gather = bf16[256,256]{1,0:T(8,128)(2,1)S(1)} all-gather(bf16[32,256]{1,0:T(8,128)(2,1)S(1)} %gather_fusion.1), channel_id=2, replica_groups=mesh['dom'=8,'tile'=4] {'dom'}, dimensions={0}, use_global_device_ids=true | all-gather | bytes 147456 | tf_op jit(solution)/shard_map/all_gather | solution.py:37
  78.2 0.1 pad_maximum_fusion
  78.3 5.6 %gather_fusion.2 = bf16[72,128,256]{2,1,0:T(8,128)(2,1)} fusion(bf16[26,128,256]{2,1,0:T(8,128)(2,1)S(1)} %bitcast.45, s32[1024]{0:T(1024)S(1)} %pad_clamp_fusion.1), kind=kCustom, calls=%fused_computation.2 | custom fusion | bytes 9437472 | tf_op jit(solution)/shard_map/gather | solution.py:43
  83.9 8.2 %convolution_bitcast_fusion.1 = f32[72,128,256]{1,2,0:T(8,128)} fusion(bf16[72,128,256]{2,1,0:T(8,128)(2,1)} %gather_fusion.2, bf16[72,128,128]{2,1,0:T(8,128)(2,1)} %param.13), kind=kOutput, calls=%fused_computation.8 | convolution fusion | flops 603979776 | bytes 16515072 | tf_op jit(solution)/shard_map/tij,tjf->tif/dot_general | solution.py:44
  92.1 9.6 %copy.33 = f32[72,128,256]{2,0,1:T(8,128)} copy(f32[72,128,256]{1,2,0:T(8,128)} %convolution_bitcast_fusion.1) | data formatting | bytes 18874368 | tf_op jit(solution)/shard_map/tij,tjf->tif/dot_general | solution.py:44
  101.7 6.9 %convolution_convert_fusion.1 = bf16[16,128,256]{2,0,1:T(8,128)(2,1)S(1)} fusion(f32[72,128,256]{2,0,1:T(8,128)} %copy.33, s32[72]{0:T(128)S(1)} %copy-done.8), kind=kOutput, calls=%fused_computation.11 | convolution fusion | flops 453510272 | bytes 10486048 | tf_op jit(solution)/shard_map/dt,tif->dif/dot_general | solution.py:46
  108.7 0.0 copy-start.3
  108.7 0.0 copy-start.4
  108.7 0.0 copy-start.6
  108.7 1.3 copy.34
  110.1 0.0 reduce-scatter.4.cloned.1.call-update
  110.1 0.0 all-gather.6.cloned.1.call-start
  110.1 0.6 dynamic-slice
  111.4 0.7 convert_reduce_fusion
  112.1 0.1 fusion.3
  112.2 5.9 %all-reduce = bf16[2048]{0:T(1024)(128)(2,1)S(1)} all-reduce(bf16[2048]{0:T(1024)(128)(2,1)S(1)} %fusion.3), channel_id=4, replica_groups=mesh['dom'=8,'tile'=4] {'tile'}, use_global_device_ids=true, to_apply=%region_2.0.clone | all-reduce | flops 2048 | bytes 8192
  118.2 0.1 convert_maximum_fusion
  118.2 0.2 fusion.15
  118.5 13.0 %reduce-scatter.4.cloned.1.call-done = bf16[512,256]{1,0:T(8,128)(2,1)} async-done(((bf16[2048,256]{1,0:T(8,128)(2,1)}), bf16[512,256]{1,0:T(8,128)(2,1)}) %reduce-scatter.4.cloned.1.call-update) | async-done | bytes 262160 | tf_op jit(solution)/shard_map/reduce_scatter | solution.py:54
  131.4 2.2 multiply_convert_fusion
  133.6 1.0 fusion.2
  134.6 0.0 all-gather.6.cloned.1.call-update
  134.6 0.2 all-reduce.5.cloned.1.call-start
  134.9 16.6 %all-gather.6.cloned.1.call-done = bf16[2048,256]{1,0:T(8,128)(2,1)} async-done(((bf16[512,256]{1,0:T(8,128)(2,1)}), bf16[2048,256]{1,0:T(8,128)(2,1)}) %all-gather.6.cloned.1.call-update) | async-done | bytes 1048592 | tf_op jit(solution)/shard_map/all_gather | solution.py:79
  151.5 6.8 %gather_fusion.3 = bf16[72,128,256]{2,1,0:T(8,128)(2,1)} fusion(bf16[16,128,256]{2,1,0:T(8,128)(2,1)} %bitcast.46, s32[1024]{0:T(1024)S(1)} %pad_clamp_fusion), kind=kCustom, calls=%fused_computation.3 | custom fusion | bytes 9437472 | tf_op jit(solution)/shard_map/gather | solution.py:80
  158.3 7.4 %convolution_bitcast_fusion = f32[72,128,256]{1,2,0:T(8,128)} fusion(bf16[72,128,256]{2,1,0:T(8,128)(2,1)} %gather_fusion.3, bf16[72,128,128]{2,1,0:T(8,128)(2,1)S(1)} %copy-done.3), kind=kOutput, calls=%fused_computation.7 | convolution fusion | flops 603979776 | bytes 16515072 | tf_op jit(solution)/shard_map/tij,tif->tjf/dot_general | solution.py:81
  165.7 9.6 %copy.36 = f32[72,128,256]{2,0,1:T(8,128)} copy(f32[72,128,256]{1,2,0:T(8,128)} %convolution_bitcast_fusion) | data formatting | bytes 18874368 | tf_op jit(solution)/shard_map/tij,tif->tjf/dot_general | solution.py:81
  175.4 7.7 %convolution_convert_fusion = bf16[26,128,256]{2,0,1:T(8,128)(2,1)S(1)} fusion(f32[72,128,256]{2,0,1:T(8,128)} %copy.36, s32[72]{0:T(128)S(1)} %copy-done.10), kind=kOutput, calls=%fused_computation.9 | convolution fusion | flops 736954176 | bytes 11141408 | tf_op jit(solution)/shard_map/st,tjf->sjf/dot_general | solution.py:83
  183.0 0.1 slice.34
  183.2 1.0 copy.38
  184.2 0.0 all-reduce.5.cloned.1.call-update
  184.2 0.0 all-reduce.7.cloned.1.call-start
  184.3 1.0 convolution_bitcast_fusion.2
  185.3 1.1 fusion.14
  186.3 0.0 all-reduce.7.cloned.1.call-update
  186.4 0.0 reduce-scatter.8.cloned.1.call-start
  186.4 31.8 %all-reduce.5.cloned.1.call-done = bf16[1280,256]{1,0:T(8,128)(2,1)} async-done(((bf16[1280,256]{1,0:T(8,128)(2,1)}), bf16[1280,256]{1,0:T(8,128)(2,1)}) %all-reduce.5.cloned.1.call-update) | async-done | bytes 655376 | tf_op jit(solution)/shard_map/psum | solution.py:89
  218.2 1.6 slice_convert_fusion
  219.8 0.0 reduce-scatter.8.cloned.1.call-update
  219.8 0.0 reduce-scatter.6.cloned.1.call-start
  219.9 0.1 slice.33
  220.0 1.3 copy.37
  221.3 0.0 reduce-scatter.6.cloned.1.call-update
  221.4 0.9 slice.35
  222.2 5.7 %all-to-all-start.1 = ((bf16[8,128,256]{2,1,0:T(8,128)(2,1)}), bf16[8,128,256]{2,1,0:T(8,128)(2,1)S(1)}, u32[]{:S(2)}, u32[]{:S(2)}) async-start(bf16[8,128,256]{2,1,0:T(8,128)(2,1)} %bitcast.14), calls=%async_computation.3 | async-start | bytes 1048576 | tf_op jit(solution)/shard_map/all_to_all | solution.py:93
  227.9 126.8 %all-reduce.7.cloned.1.call-done = (f32[256,256]{0,1:T(8,128)}, f32[256,256]{0,1:T(8,128)}) async-done(((f32[256,256]{0,1:T(8,128)}, f32[256,256]{0,1:T(8,128)}), (f32[256,256]{0,1:T(8,128)}, f32[256,256]{0,1:T(8,128)})) %all-reduce.7.cloned.1.call-update) | async-done | bytes 524304 | tf_op jit(solution)/shard_map/psum | solution.py:73
  354.7 1.1 broadcast_multiply_fusion
  355.8 0.8 copy.40
  356.6 0.8 copy.41
  357.5 6.6 %scatter_custom_fusion = f32[2048,256]{1,0:T(8,128)S(1)} fusion(s32[1024]{0:T(1024)S(1)} %bitcast.53, bf16[1024,256]{1,0:T(8,128)(2,1)S(1)} %bitcast.50, f32[]{:T(128)} %constant.12.clone.1), kind=kCustom, calls=%fused_computation.21 | custom fusion | flops 524288 | bytes 2621444 | tf_op jit(solution)/shard_map/scatter-add | solution.py:100
  364.1 54.6 %reduce-scatter.8.cloned.1.call-done = f32[32,256]{1,0:T(8,128)} async-done(((f32[256,256]{1,0:T(8,128)}), f32[32,256]{1,0:T(8,128)}) %reduce-scatter.8.cloned.1.call-update) | async-done | bytes 32784 | tf_op jit(solution)/shard_map/reduce_scatter | solution.py:99
  418.7 1.8 scatter_fusion
  420.5 24.7 %reduce-scatter.6.cloned.1.call-done = bf16[512,256]{1,0:T(8,128)(2,1)} async-done(((bf16[2048,256]{1,0:T(8,128)(2,1)}), bf16[512,256]{1,0:T(8,128)(2,1)}) %reduce-scatter.6.cloned.1.call-update) | async-done | bytes 262160 | tf_op jit(solution)/shard_map/reduce_scatter | solution.py:86
  445.2 1.9 fusion.1
  (32 shorter events, 0.1 us)
Async XLA Ops:
  7.2 124.3 %copy-start = (bf16[256,256]{1,0:T(8,128)(2,1)S(1)}, bf16[256,256]{1,0:T(8,128)(2,1)}, u32[]{:S(2)}) copy-start(bf16[256,256]{1,0:T(8,128)(2,1)} %param.12) | copy-start | bytes 393220
  7.2 33.5 %copy-start.12 = (s32[32]{0:T(128)S(1)}, s32[32]{0:T(128)}, u32[]{:S(2)}) copy-start(s32[32]{0:T(128)} %param.17) | copy-start | bytes 388
  7.2 33.5 %copy-start.9 = (s32[72]{0:T(128)S(1)}, s32[72]{0:T(128)}, u32[]{:S(2)}) copy-start(s32[72]{0:T(128)} %param.15) | copy-start | bytes 868
  7.2 21.8 %all-gather.4.cloned.1.call-start = ((), (), s32[]{:S(2)}) async-start(), calls=%async_computation.5 | async-start | bytes 1310720 | tf_op jit(solution)/shard_map/all_gather | solution.py:29
  29.1 11.7 %copy-start.2 = (bf16[2048,256]{1,0:T(8,128)(2,1)S(1)}, bf16[2048,256]{1,0:T(8,128)(2,1)}, u32[]{:S(2)}) copy-start(bf16[2048,256]{1,0:T(8,128)(2,1)} %all-gather.4.cloned.1.call-done) | copy-start | bytes 3145732
  35.1 43.1 %all-to-all-start = ((bf16[8,128,256]{2,1,0:T(8,128)(2,1)}), bf16[8,128,256]{2,1,0:T(8,128)(2,1)S(1)}, u32[]{:S(2)}, u32[]{:S(2)}) async-start(bf16[8,128,256]{2,1,0:T(8,128)(2,1)} %bitcast.3), calls=%async_computation | async-start | bytes 1048576 | tf_op jit(solution)/shard_map/all_to_all | solution.py:34
  40.6 90.8 %reduce-scatter.4.cloned.1.call-start = ((), (), s32[]{:S(2)}) async-start(), calls=%async_computation.6 | async-start | bytes 1310720 | tf_op jit(solution)/shard_map/reduce_scatter | solution.py:54
  92.1 9.6 %copy-start.8 = (s32[72]{0:T(128)S(1)}, s32[72]{0:T(128)}, u32[]{:S(2)}) copy-start(s32[72]{0:T(128)} %param.14) | copy-start | bytes 868
  101.7 8.4 %copy-start.13 = (u32[32]{0:T(128)S(1)}, u32[32]{0:T(128)}, u32[]{:S(2)}) copy-start(u32[32]{0:T(128)} %constant.8) | copy-start | bytes 388
  108.7 2.7 copy-start.3
  108.7 9.5 %copy-start.4 = (bf16[512,256]{1,0:T(8,128)(2,1)S(1)}, bf16[512,256]{1,0:T(8,128)(2,1)}, u32[]{:S(2)}) copy-start(bf16[512,256]{1,0:T(8,128)(2,1)} %param.9) | copy-start | bytes 786436
  108.7 9.5 %copy-start.6 = (bf16[256,256]{1,0:T(8,128)(2,1)S(1)}, bf16[256,256]{1,0:T(8,128)(2,1)}, u32[]{:S(2)}) copy-start(bf16[256,256]{1,0:T(8,128)(2,1)} %param.11) | copy-start | bytes 393220
  110.1 41.4 %all-gather.6.cloned.1.call-start = ((), (), s32[]{:S(2)}) async-start(), calls=%async_computation.7 | async-start | bytes 1310720 | tf_op jit(solution)/shard_map/all_gather | solution.py:79
  134.6 83.6 %all-reduce.5.cloned.1.call-start = ((), (), s32[]{:S(2)}) async-start(), calls=%async_computation.9 | async-start | bytes 1310720 | tf_op jit(solution)/shard_map/psum | solution.py:89
  165.7 9.6 %copy-start.10 = (s32[72]{0:T(128)S(1)}, s32[72]{0:T(128)}, u32[]{:S(2)}) copy-start(s32[72]{0:T(128)} %param.15) | copy-start | bytes 868
  183.0 2.2 copy-start.11
  184.2 170.5 %all-reduce.7.cloned.1.call-start = ((), (), s32[]{:S(2)}) async-start(), calls=%async_computation.11 | async-start | bytes 1048576 | tf_op jit(solution)/shard_map/psum | solution.py:73
  186.4 232.4 %reduce-scatter.8.cloned.1.call-start = ((), (), s32[]{:S(2)}) async-start(), calls=%async_computation.10 | async-start | bytes 294912 | tf_op jit(solution)/shard_map/reduce_scatter | solution.py:99
  219.8 225.3 %reduce-scatter.6.cloned.1.call-start = ((), (), s32[]{:S(2)}) async-start(), calls=%async_computation.8 | async-start | bytes 1310720 | tf_op jit(solution)/shard_map/reduce_scatter | solution.py:86
  220.0 1.4 copy-start.5
  222.2 223.0 %copy-start.7 = (bf16[256,256]{1,0:T(8,128)(2,1)S(1)}, bf16[256,256]{1,0:T(8,128)(2,1)}, u32[]{:S(2)}) copy-start(bf16[256,256]{1,0:T(8,128)(2,1)} %param.11) | copy-start | bytes 393220
  222.2 135.2 %all-to-all-start.1 = ((bf16[8,128,256]{2,1,0:T(8,128)(2,1)}), bf16[8,128,256]{2,1,0:T(8,128)(2,1)S(1)}, u32[]{:S(2)}, u32[]{:S(2)}) async-start(bf16[8,128,256]{2,1,0:T(8,128)(2,1)} %bitcast.14), calls=%async_computation.3 | async-start | bytes 1048576 | tf_op jit(solution)/shard_map/all_to_all | solution.py:93
  227.9 219.2 %copy-start.1 = (bf16[256,256]{1,0:T(8,128)(2,1)S(1)}, bf16[256,256]{1,0:T(8,128)(2,1)}, u32[]{:S(2)}) copy-start(bf16[256,256]{1,0:T(8,128)(2,1)} %param.12) | copy-start | bytes 393220
Sparse Core Ops, SparseCore 0:
  9.6 19.4 all-gather.3
  110.2 21.1 reduce-scatter.3
  134.7 16.7 all-gather.5
  184.4 33.7 all-reduce.4
  225.0 129.7 all-reduce.6
  358.5 60.1 reduce-scatter.7
  421.2 23.9 reduce-scatter.5
where the time goes:
time: 455 us; the launch traced here: 454 us
  waiting for transfers between devices  289 us (64%)
  local copies, waits for them, and re-layouts  45.4 us (10%)
  blocking collectives  42.8 us (9%)
  matrix products  37.7 us (8%)
  between operations  15 us (3%)
  other arithmetic  12.7 us (3%)
  starting transfers between devices  11.6 us (3%)
    psum x1, waiting for transfers between devices, on_device(): lax.psum((self_term, neigh_term), ('dom', 'tile'))  127 us
    reduce_scatter x1, waiting for transfers between devices, on_device(): lax.psum_scatter(hub_grad, 'dom', scatter_dimension=0, tiled=True)  54.6 us
    all_gather x1, blocking collectives, on_device(): hub_rows = lax.all_gather(own_hubs, 'dom', axis=0, tiled=True)  36.8 us
    psum x1, waiting for transfers between devices, on_device(): lax.psum(partial_src[vertices:].astype(jnp.bfloat16), 'tile')  31.8 us
    reduce_scatter x1, waiting for transfers between devices, on_device(): lax.psum_scatter(partial_src[:vertices].astype(jnp.bfloat16), 'tile', sca...  24.7 us
    all_gather x1, waiting for transfers between devices, on_device(): whole_rows = lax.all_gather(features, 'tile', axis=0, tiled=True)  20.4 us
    all_gather x1, waiting for transfers between devices, on_device(): grad_whole = lax.all_gather(grad_mean_b, 'tile', axis=0, tiled=True)  16.6 us
    reduce_scatter x1, waiting for transfers between devices, on_device(): lax.psum_scatter(partial_sum.astype(jnp.bfloat16), 'tile', scatter_dimens...  13 us
  transfers between devices with their start and end apart: 9, of which 7 were waited for; matrix products, arithmetic and copies ran while one was open for 4% of the time, Pallas kernels for 0%

commit v1 on v0

--- a/solution.py
+++ b/solution.py
@@ -70,7 +70,7 @@
     ).astype(jnp.bfloat16)
     self_term = jnp.einsum("nf,nh->fh", features, grad_hidden, preferred_element_type=jnp.float32)
     neigh_term = jnp.einsum("nf,nh->fh", mean_rows, grad_hidden, preferred_element_type=jnp.float32)
-    grad_self_sum, grad_neigh_sum = lax.psum((self_term, neigh_term), ("dom", "tile"))
+    grad_self_sum, grad_neigh_sum = lax.psum(lax.psum((self_term, neigh_term), "tile"), "dom")
     inv_root = 1.0 / (quarter * groups * domains) ** 0.5
     grad_mean = lax.dot_general(
         grad_hidden, neigh_weight, (((1,), (1,)), ((), ())), preferred_element_type=jnp.float32

time: 455 us -> 406 us (0.89)
  waiting for transfers between devices: 289 us -> 238 us
    psum x1 -> x2, waiting for transfers between devices: 127 us -> 74.5 us  [the longest x1 71.3 us: on_device(): lax.psum(lax.psum((self_term, neigh_term), 'tile'), 'dom')]
  transfers between devices with their start and end apart: 9 -> 10, of which waited for: 7 -> 8; matrix products, arithmetic and copies ran while one was open for 4% -> 13% of each run, Pallas kernels for 0% -> 0%
where the time goes in v1:
time: 406 us; the launch traced here: 405 us
  waiting for transfers between devices  238 us (59%)
  local copies, waits for them, and re-layouts  45.6 us (11%)
  blocking collectives  42.8 us (11%)
  matrix products  38.8 us (10%)
  between operations  15 us (4%)
  other arithmetic  12.7 us (3%)
  starting transfers between devices  11.7 us (3%)
    psum x1, waiting for transfers between devices, on_device(): lax.psum(lax.psum((self_term, neigh_term), 'tile'), 'dom')  71.3 us
    reduce_scatter x1, waiting for transfers between devices, on_device(): lax.psum_scatter(hub_grad, 'dom', scatter_dimension=0, tiled=True)  55 us
    all_gather x1, blocking collectives, on_device(): hub_rows = lax.all_gather(own_hubs, 'dom', axis=0, tiled=True)  36.8 us
    psum x1, waiting for transfers between devices, on_device(): lax.psum(partial_src[vertices:].astype(jnp.bfloat16), 'tile')  36.2 us
    reduce_scatter x1, waiting for transfers between devices, on_device(): lax.psum_scatter(partial_src[:vertices].astype(jnp.bfloat16), 'tile', sca...  24.7 us
    all_gather x1, waiting for transfers between devices, on_device(): whole_rows = lax.all_gather(features, 'tile', axis=0, tiled=True)  20.4 us
    all_gather x1, waiting for transfers between devices, on_device(): grad_whole = lax.all_gather(grad_mean_b, 'tile', axis=0, tiled=True)  13.6 us
    reduce_scatter x1, waiting for transfers between devices, on_device(): lax.psum_scatter(partial_sum.astype(jnp.bfloat16), 'tile', scatter_dimens...  13 us
  transfers between devices with their start and end apart: 10, of which 8 were waited for; matrix products, arithmetic and copies ran while one was open for 13% of the time, Pallas kernels for 0%

profile of v1, /device:TPU:0, one launch (start us, length us, event | category | flops | bytes accessed | tf_op | source)
XLA Modules:
  0.0 404.8 jit_solution(15349282896546801248)
XLA Ops:
  7.2 0.0 copy-start
  7.2 0.0 copy-start.9
  7.2 0.0 all-gather.4.cloned.1.call-start
  7.3 0.7 all-gather.4.cloned.1.call-update
  7.9 0.7 compare_select_fusion
  8.6 20.4 %all-gather.4.cloned.1.call-done = bf16[2048,256]{1,0:T(8,128)(2,1)} async-done(((bf16[512,256]{1,0:T(8,128)(2,1)}), bf16[2048,256]{1,0:T(8,128)(2,1)}) %all-gather.4.cloned.1.call-update) | async-done | bytes 1048592 | tf_op jit(solution)/shard_map/all_gather | solution.py:29
  29.1 6.0 %gather_fusion = bf16[1024,256]{1,0:T(8,128)(2,1)} fusion(bf16[2048,256]{1,0:T(8,128)(2,1)} %all-gather.4.cloned.1.call-done, s32[1024]{0:T(1024)S(1)} %broadcast_clamp_fusion), kind=kCustom, calls=%fused_computation | custom fusion | bytes 1052672 | tf_op jit(solution)/shard_map/gather | solution.py:31
  35.1 5.5 %all-to-all-start = ((bf16[8,128,256]{2,1,0:T(8,128)(2,1)}), bf16[8,128,256]{2,1,0:T(8,128)(2,1)S(1)}, u32[]{:S(2)}, u32[]{:S(2)}) async-start(bf16[8,128,256]{2,1,0:T(8,128)(2,1)} %bitcast.3), calls=%async_computation | async-start | bytes 1048576 | tf_op jit(solution)/shard_map/all_to_all | solution.py:34
  40.6 0.0 reduce-scatter.4.cloned.1.call-start
  40.7 0.6 gather_fusion.1
  41.3 36.8 %all-gather = bf16[256,256]{1,0:T(8,128)(2,1)S(1)} all-gather(bf16[32,256]{1,0:T(8,128)(2,1)S(1)} %gather_fusion.1), channel_id=2, replica_groups=mesh['dom'=8,'tile'=4] {'dom'}, dimensions={0}, use_global_device_ids=true | all-gather | bytes 147456 | tf_op jit(solution)/shard_map/all_gather | solution.py:37
  78.2 0.1 pad_maximum_fusion
  78.3 5.6 %gather_fusion.2 = bf16[72,128,256]{2,1,0:T(8,128)(2,1)} fusion(bf16[26,128,256]{2,1,0:T(8,128)(2,1)S(1)} %bitcast.45, s32[1024]{0:T(1024)S(1)} %pad_clamp_fusion.1), kind=kCustom, calls=%fused_computation.2 | custom fusion | bytes 9437472 | tf_op jit(solution)/shard_map/gather | solution.py:43
  83.9 8.2 %convolution_bitcast_fusion.1 = f32[72,128,256]{1,2,0:T(8,128)} fusion(bf16[72,128,256]{2,1,0:T(8,128)(2,1)} %gather_fusion.2, bf16[72,128,128]{2,1,0:T(8,128)(2,1)} %param.13), kind=kOutput, calls=%fused_computation.8 | convolution fusion | flops 603979776 | bytes 16515072 | tf_op jit(solution)/shard_map/tij,tjf->tif/dot_general | solution.py:44
  92.1 9.7 %copy.33 = f32[72,128,256]{2,0,1:T(8,128)} copy(f32[72,128,256]{1,2,0:T(8,128)} %convolution_bitcast_fusion.1) | data formatting | bytes 18874368 | tf_op jit(solution)/shard_map/tij,tjf->tif/dot_general | solution.py:44
  101.8 6.9 %convolution_convert_fusion.1 = bf16[16,128,256]{2,0,1:T(8,128)(2,1)S(1)} fusion(f32[72,128,256]{2,0,1:T(8,128)} %copy.33, s32[72]{0:T(128)S(1)} %copy-done.8), kind=kOutput, calls=%fused_computation.11 | convolution fusion | flops 453510272 | bytes 10486048 | tf_op jit(solution)/shard_map/dt,tif->dif/dot_general | solution.py:46
  108.8 1.3 copy.34
  110.1 0.0 reduce-scatter.4.cloned.1.call-update
  110.2 0.0 all-gather.6.cloned.1.call-start
  110.2 0.6 dynamic-slice
  111.5 0.7 convert_reduce_fusion
  112.2 0.1 fusion.3
  112.3 5.9 %all-reduce = bf16[2048]{0:T(1024)(128)(2,1)S(1)} all-reduce(bf16[2048]{0:T(1024)(128)(2,1)S(1)} %fusion.3), channel_id=4, replica_groups=mesh['dom'=8,'tile'=4] {'tile'}, use_global_device_ids=true, to_apply=%region_2.0.clone | all-reduce | flops 2048 | bytes 8192
  118.2 0.1 convert_maximum_fusion
  118.3 0.2 fusion.15
  118.5 13.0 %reduce-scatter.4.cloned.1.call-done = bf16[512,256]{1,0:T(8,128)(2,1)} async-done(((bf16[2048,256]{1,0:T(8,128)(2,1)}), bf16[512,256]{1,0:T(8,128)(2,1)}) %reduce-scatter.4.cloned.1.call-update) | async-done | bytes 262160 | tf_op jit(solution)/shard_map/reduce_scatter | solution.py:54
  131.5 2.2 multiply_convert_fusion
  133.7 1.0 fusion.2
  134.7 0.0 all-gather.6.cloned.1.call-update
  134.7 0.0 all-reduce.11.cloned.1.call-start
  134.8 1.0 convolution_bitcast_fusion.2
  135.7 2.0 fusion.14
  137.8 0.0 all-reduce.11.cloned.1.call-update
  137.8 0.2 all-reduce.7.cloned.1.call-start
  138.0 13.6 %all-gather.6.cloned.1.call-done = bf16[2048,256]{1,0:T(8,128)(2,1)} async-done(((bf16[512,256]{1,0:T(8,128)(2,1)}), bf16[2048,256]{1,0:T(8,128)(2,1)}) %all-gather.6.cloned.1.call-update) | async-done | bytes 1048592 | tf_op jit(solution)/shard_map/all_gather | solution.py:79
  151.6 6.8 %gather_fusion.3 = bf16[72,128,256]{2,1,0:T(8,128)(2,1)} fusion(bf16[16,128,256]{2,1,0:T(8,128)(2,1)} %bitcast.46, s32[1024]{0:T(1024)S(1)} %pad_clamp_fusion), kind=kCustom, calls=%fused_computation.3 | custom fusion | bytes 9437472 | tf_op jit(solution)/shard_map/gather | solution.py:80
  158.4 7.5 %convolution_bitcast_fusion = f32[72,128,256]{1,2,0:T(8,128)} fusion(bf16[72,128,256]{2,1,0:T(8,128)(2,1)} %gather_fusion.3, bf16[72,128,128]{2,1,0:T(8,128)(2,1)S(1)} %copy-done.3), kind=kOutput, calls=%fused_computation.7 | convolution fusion | flops 603979776 | bytes 16515072 | tf_op jit(solution)/shard_map/tij,tif->tjf/dot_general | solution.py:81
  165.9 9.7 %copy.36 = f32[72,128,256]{2,0,1:T(8,128)} copy(f32[72,128,256]{1,2,0:T(8,128)} %convolution_bitcast_fusion) | data formatting | bytes 18874368 | tf_op jit(solution)/shard_map/tij,tif->tjf/dot_general | solution.py:81
  175.6 7.8 %convolution_convert_fusion = bf16[26,128,256]{2,0,1:T(8,128)(2,1)S(1)} fusion(f32[72,128,256]{2,0,1:T(8,128)} %copy.36, s32[72]{0:T(128)S(1)} %copy-done.10), kind=kOutput, calls=%fused_computation.9 | convolution fusion | flops 736954176 | bytes 11141408 | tf_op jit(solution)/shard_map/st,tjf->sjf/dot_general | solution.py:83
  183.4 0.1 slice.34
  183.6 1.0 copy.38
  184.6 0.0 all-reduce.7.cloned.1.call-update
  184.6 0.0 all-reduce.9.cloned.1.call-start
  184.7 3.2 all-reduce.11.cloned.1.call-done
  187.8 0.0 all-reduce.9.cloned.1.call-update
  187.9 0.0 reduce-scatter.8.cloned.1.call-start
  187.9 36.2 %all-reduce.7.cloned.1.call-done = bf16[1280,256]{1,0:T(8,128)(2,1)} async-done(((bf16[1280,256]{1,0:T(8,128)(2,1)}), bf16[1280,256]{1,0:T(8,128)(2,1)}) %all-reduce.7.cloned.1.call-update) | async-done | bytes 655376 | tf_op jit(solution)/shard_map/psum | solution.py:89
  224.2 1.6 slice_convert_fusion
  225.8 0.0 reduce-scatter.8.cloned.1.call-update
  225.8 0.0 reduce-scatter.6.cloned.1.call-start
  225.9 0.1 slice.33
  226.0 1.3 copy.37
  227.3 0.0 reduce-scatter.6.cloned.1.call-update
  227.3 0.9 slice.35
  228.2 5.6 %all-to-all-start.1 = ((bf16[8,128,256]{2,1,0:T(8,128)(2,1)}), bf16[8,128,256]{2,1,0:T(8,128)(2,1)S(1)}, u32[]{:S(2)}, u32[]{:S(2)}) async-start(bf16[8,128,256]{2,1,0:T(8,128)(2,1)} %bitcast.14), calls=%async_computation.3 | async-start | bytes 1048576 | tf_op jit(solution)/shard_map/all_to_all | solution.py:93
  233.9 71.3 %all-reduce.9.cloned.1.call-done = (f32[256,256]{0,1:T(8,128)}, f32[256,256]{0,1:T(8,128)}) async-done(((f32[256,256]{0,1:T(8,128)}, f32[256,256]{0,1:T(8,128)}), (f32[256,256]{0,1:T(8,128)}, f32[256,256]{0,1:T(8,128)})) %all-reduce.9.cloned.1.call-update) | async-done | bytes 524304 | tf_op jit(solution)/shard_map/psum | solution.py:73
  305.2 1.1 broadcast_multiply_fusion
  306.2 0.8 copy.40
  307.1 0.8 copy.41
  307.9 6.6 %scatter_custom_fusion = f32[2048,256]{1,0:T(8,128)S(1)} fusion(s32[1024]{0:T(1024)S(1)} %bitcast.53, bf16[1024,256]{1,0:T(8,128)(2,1)S(1)} %bitcast.50, f32[]{:T(128)} %constant.12.clone.1), kind=kCustom, calls=%fused_computation.21 | custom fusion | flops 524288 | bytes 2621444 | tf_op jit(solution)/shard_map/scatter-add | solution.py:100
  314.5 55.0 %reduce-scatter.8.cloned.1.call-done = f32[32,256]{1,0:T(8,128)} async-done(((f32[256,256]{1,0:T(8,128)}), f32[32,256]{1,0:T(8,128)}) %reduce-scatter.8.cloned.1.call-update) | async-done | bytes 32784 | tf_op jit(solution)/shard_map/reduce_scatter | solution.py:99
  369.5 1.8 scatter_fusion
  371.3 24.7 %reduce-scatter.6.cloned.1.call-done = bf16[512,256]{1,0:T(8,128)(2,1)} async-done(((bf16[2048,256]{1,0:T(8,128)(2,1)}), bf16[512,256]{1,0:T(8,128)(2,1)}) %reduce-scatter.6.cloned.1.call-update) | async-done | bytes 262160 | tf_op jit(solution)/shard_map/reduce_scatter | solution.py:86
  396.0 1.9 fusion.1
  (33 shorter events, 0.1 us)
Async XLA Ops:
  7.2 124.3 %copy-start = (bf16[256,256]{1,0:T(8,128)(2,1)S(1)}, bf16[256,256]{1,0:T(8,128)(2,1)}, u32[]{:S(2)}) copy-start(bf16[256,256]{1,0:T(8,128)(2,1)} %param.12) | copy-start | bytes 393220
  7.2 33.5 %copy-start.11 = (s32[32]{0:T(128)S(1)}, s32[32]{0:T(128)}, u32[]{:S(2)}) copy-start(s32[32]{0:T(128)} %param.17) | copy-start | bytes 388
  7.2 33.5 %copy-start.9 = (s32[72]{0:T(128)S(1)}, s32[72]{0:T(128)}, u32[]{:S(2)}) copy-start(s32[72]{0:T(128)} %param.15) | copy-start | bytes 868
  7.2 21.8 %all-gather.4.cloned.1.call-start = ((), (), s32[]{:S(2)}) async-start(), calls=%async_computation.5 | async-start | bytes 1310720 | tf_op jit(solution)/shard_map/all_gather | solution.py:29
  29.1 11.7 %copy-start.2 = (bf16[2048,256]{1,0:T(8,128)(2,1)S(1)}, bf16[2048,256]{1,0:T(8,128)(2,1)}, u32[]{:S(2)}) copy-start(bf16[2048,256]{1,0:T(8,128)(2,1)} %all-gather.4.cloned.1.call-done) | copy-start | bytes 3145732
  35.1 43.1 %all-to-all-start = ((bf16[8,128,256]{2,1,0:T(8,128)(2,1)}), bf16[8,128,256]{2,1,0:T(8,128)(2,1)S(1)}, u32[]{:S(2)}, u32[]{:S(2)}) async-start(bf16[8,128,256]{2,1,0:T(8,128)(2,1)} %bitcast.3), calls=%async_computation | async-start | bytes 1048576 | tf_op jit(solution)/shard_map/all_to_all | solution.py:34
  40.6 90.9 %reduce-scatter.4.cloned.1.call-start = ((), (), s32[]{:S(2)}) async-start(), calls=%async_computation.6 | async-start | bytes 1310720 | tf_op jit(solution)/shard_map/reduce_scatter | solution.py:54
  92.1 9.7 %copy-start.8 = (s32[72]{0:T(128)S(1)}, s32[72]{0:T(128)}, u32[]{:S(2)}) copy-start(s32[72]{0:T(128)} %param.14) | copy-start | bytes 868
  101.8 8.4 %copy-start.12 = (u32[32]{0:T(128)S(1)}, u32[32]{0:T(128)}, u32[]{:S(2)}) copy-start(u32[32]{0:T(128)} %constant.8) | copy-start | bytes 388
  108.7 2.7 copy-start.3
  108.8 9.6 %copy-start.4 = (bf16[512,256]{1,0:T(8,128)(2,1)S(1)}, bf16[512,256]{1,0:T(8,128)(2,1)}, u32[]{:S(2)}) copy-start(bf16[512,256]{1,0:T(8,128)(2,1)} %param.9) | copy-start | bytes 786436
  108.8 9.5 %copy-start.6 = (bf16[256,256]{1,0:T(8,128)(2,1)S(1)}, bf16[256,256]{1,0:T(8,128)(2,1)}, u32[]{:S(2)}) copy-start(bf16[256,256]{1,0:T(8,128)(2,1)} %param.11) | copy-start | bytes 393220
  110.2 41.4 %all-gather.6.cloned.1.call-start = ((), (), s32[]{:S(2)}) async-start(), calls=%async_computation.7 | async-start | bytes 1310720 | tf_op jit(solution)/shard_map/all_gather | solution.py:79
  134.7 53.1 %all-reduce.11.cloned.1.call-start = ((), (), s32[]{:S(2)}) async-start(), calls=%async_computation.12 | async-start | bytes 1048576 | tf_op jit(solution)/shard_map/psum | solution.py:73
  137.8 86.4 %all-reduce.7.cloned.1.call-start = ((), (), s32[]{:S(2)}) async-start(), calls=%async_computation.9 | async-start | bytes 1310720 | tf_op jit(solution)/shard_map/psum | solution.py:89
  165.9 9.8 %copy-start.10 = (s32[72]{0:T(128)S(1)}, s32[72]{0:T(128)}, u32[]{:S(2)}) copy-start(s32[72]{0:T(128)} %param.15) | copy-start | bytes 868
  184.6 120.5 %all-reduce.9.cloned.1.call-start = ((), (), s32[]{:S(2)}) async-start(), calls=%async_computation.11 | async-start | bytes 1048576 | tf_op jit(solution)/shard_map/psum | solution.py:73
  187.9 181.7 %reduce-scatter.8.cloned.1.call-start = ((), (), s32[]{:S(2)}) async-start(), calls=%async_computation.10 | async-start | bytes 294912 | tf_op jit(solution)/shard_map/reduce_scatter | solution.py:99
  225.8 170.2 %reduce-scatter.6.cloned.1.call-start = ((), (), s32[]{:S(2)}) async-start(), calls=%async_computation.8 | async-start | bytes 1310720 | tf_op jit(solution)/shard_map/reduce_scatter | solution.py:86
  226.0 1.4 copy-start.5
  228.2 167.8 %copy-start.7 = (bf16[256,256]{1,0:T(8,128)(2,1)S(1)}, bf16[256,256]{1,0:T(8,128)(2,1)}, u32[]{:S(2)}) copy-start(bf16[256,256]{1,0:T(8,128)(2,1)} %param.11) | copy-start | bytes 393220
  228.2 79.7 %all-to-all-start.1 = ((bf16[8,128,256]{2,1,0:T(8,128)(2,1)}), bf16[8,128,256]{2,1,0:T(8,128)(2,1)S(1)}, u32[]{:S(2)}, u32[]{:S(2)}) async-start(bf16[8,128,256]{2,1,0:T(8,128)(2,1)} %bitcast.14), calls=%async_computation.3 | async-start | bytes 1048576 | tf_op jit(solution)/shard_map/all_to_all | solution.py:93
  233.8 164.1 %copy-start.1 = (bf16[256,256]{1,0:T(8,128)(2,1)S(1)}, bf16[256,256]{1,0:T(8,128)(2,1)}, u32[]{:S(2)}) copy-start(bf16[256,256]{1,0:T(8,128)(2,1)} %param.12) | copy-start | bytes 393220
Sparse Core Ops, SparseCore 0:
  9.6 19.4 all-gather.3
  110.3 21.1 reduce-scatter.3
  134.8 16.7 all-gather.5
  154.6 33.2 all-reduce.10
  190.2 33.9 all-reduce.6
  227.9 77.2 all-reduce.8
  309.1 60.4 reduce-scatter.7
  372.1 23.9 reduce-scatter.5
